TPU v7x, 32 devices: a whole 2x2x4 slice. The times are simulated.
32 devices in a mesh: groups: 1, expert: 16 (over z, y, core), section: 2 (over x), dp: 1.
Axes of the slice: x: 2, y: 2, z: 4, core: 2. Of those that a mesh axis runs over, the one named last changes fastest.
Arguments:
- saved_input: bfloat16 [2, 2048, 1440], P('section', ('groups', 'expert')), may hold values from -6 to 6
- grad_output: bfloat16 [2, 2048, 1440], P('section', ('groups', 'expert')), may hold values from -6 to 6
- expert_ids: int32 [2, 2048, 4], P('section', ('groups', 'expert')), may hold values from 0 to 7, all different within a row; in each aligned block of 128 rows (0 to 127, 128 to 255, ..., all dimensions but the last counted through in order) at most 68 rows name the same one
- router_logits: float32 [2, 2048, 4], P('section', ('groups', 'expert')), may hold values from -6 to 6
- w_gate: bfloat16 [2, 16, 1440, 720], P('section', 'expert', None, 'dp'), may hold values from -0.15625 to 0.15625
- w_up: bfloat16 [2, 16, 1440, 720], P('section', 'expert', None, 'dp'), may hold values from -0.15625 to 0.15625
- w_down: bfloat16 [2, 16, 720, 1440], P('section', 'expert', 'dp'), may hold values from -0.15625 to 0.15625
Outputs:
- passed: bfloat16 [2, 2048, 1440], P('section', ('groups', 'expert'))
Inputs may be any that keep to these rules, and one draw needn't show every extreme that they name: `expert_ids`: in each aligned block of 128 tokens (the tokens of one index of the expert axis) of a layer, no expert is named by more than 68 entries, a bound that some block reaches. A token names 4 different experts.
All inputs are finite; a program needn't handle non-finite values.
Results may differ from a plain program's by a relative error of at most 0.0057.
Values may be sent and summed in bfloat16 or wider, within the bound.
A program may use at most 64 MiB of HBM per device.

v0:
```python
import jax
import jax.numpy as jnp
from jax import lax
from jax.sharding import PartitionSpec as P

swish_alpha = 1.702


def swapped(value, axis, stride):
    mask = 2**stride
    pairs = [(source, source ^ mask) for source in range(lax.axis_size(axis))]
    return lax.ppermute(value, axis, pairs)


def shifted(block, axis, distance):
    devices = range(lax.axis_size(axis))
    route = [((i - distance) % len(devices), i) for i in devices]
    return lax.ppermute(block, axis, route)


def expert_rows(feat_rows, grad_rows, gate_mat, up_mat, down_mat):
    gate_pre = jnp.dot(feat_rows, gate_mat, preferred_element_type=jnp.float32)
    up_pre = jnp.dot(feat_rows, up_mat, preferred_element_type=jnp.float32)
    hidden_grad = lax.dot_general(
        grad_rows, down_mat, (((1,), (1,)), ((), ())), preferred_element_type=jnp.float32
    )
    squash = jax.nn.sigmoid(swish_alpha * gate_pre)
    slope = squash + swish_alpha * gate_pre * squash * (1.0 - squash)
    gate_grad = (hidden_grad * (up_pre + 1.0) * slope).astype(jnp.bfloat16)
    up_grad = (hidden_grad * gate_pre * squash).astype(jnp.bfloat16)
    first = lax.dot_general(
        gate_grad, gate_mat, (((1,), (1,)), ((), ())), preferred_element_type=jnp.float32
    )
    second = lax.dot_general(
        up_grad, up_mat, (((1,), (1,)), ((), ())), preferred_element_type=jnp.float32
    )
    return first + second


def on_device(saved_input, grad_output, expert_ids, router_logits, w_gate, w_up, w_down):
    gate_half = w_gate[0, 0]
    up_half = w_up[0, 0]
    down_half = w_down[0, 0]
    feat_rows = saved_input[0]
    grad_rows = grad_output[0]
    chosen = expert_ids[0]
    logits = router_logits[0]
    tokens, features = feat_rows.shape
    top_count = chosen.shape[1]
    slices = lax.axis_size("expert")
    experts = slices // 2
    capacity = min(tokens, tokens * top_count // experts * 17 // 16 // 2 * 2)
    half_cap = capacity // 2
    entries = chosen.reshape(-1)
    total_items = entries.shape[0]
    onehot = (entries[:, None] == jnp.arange(experts, dtype=jnp.int32)[None, :]).astype(jnp.int32)
    before = jnp.cumsum(onehot, axis=0) - onehot
    position = jnp.sum(before * onehot, axis=1)
    slot_of_item = entries * capacity + position
    item_of_slot = jnp.full((experts * capacity,), total_items, jnp.int32)
    item_of_slot = item_of_slot.at[slot_of_item].set(jnp.arange(total_items, dtype=jnp.int32))
    occupied = (item_of_slot < total_items)[:, None]
    source = jnp.where(item_of_slot < total_items, item_of_slot // top_count, 0)
    zero_value = jnp.zeros((), jnp.bfloat16)
    send_feats = jnp.where(occupied, feat_rows[source], zero_value).reshape(
        experts, capacity, features
    )
    send_grads = jnp.where(occupied, grad_rows[source], zero_value).reshape(
        experts, capacity, features
    )
    other_gate, other_up, other_down = swapped((gate_half, up_half, down_half), "expert", 0)
    gate_whole = jnp.concatenate([gate_half, other_gate], axis=1)
    up_whole = jnp.concatenate([up_half, other_up], axis=1)
    down_whole = jnp.concatenate([down_half, other_down], axis=0)
    split_feats = send_feats.reshape(slices, half_cap, features)
    split_grads = send_grads.reshape(slices, half_cap, features)
    got_feats = lax.all_to_all(split_feats, "expert", split_axis=0, concat_axis=0, tiled=True)
    got_grads = lax.all_to_all(split_grads, "expert", split_axis=0, concat_axis=0, tiled=True)
    senders, depth, _ = got_feats.shape
    result = expert_rows(
        got_feats.reshape(-1, features),
        got_grads.reshape(-1, features),
        gate_whole,
        up_whole,
        down_whole,
    )
    result = lax.psum(result, "dp").astype(jnp.bfloat16).reshape(senders, depth, features)
    arrived = lax.all_to_all(result, "expert", split_axis=0, concat_axis=0, tiled=True)
    slot_grad = arrived.reshape(experts * capacity, features)
    picked = slot_grad[slot_of_item].reshape(tokens, top_count, features).astype(jnp.float32)
    raised = jnp.exp(logits)
    weights = raised / jnp.sum(raised, axis=1, keepdims=True)
    combined = jnp.sum(weights[:, :, None] * picked, axis=1).astype(jnp.bfloat16)
    passed = shifted(combined, "section", -1)
    return passed[None]


def solution(mesh):
    placed = (
        P("section", ("groups", "expert"), None),
        P("section", ("groups", "expert"), None),
        P("section", ("groups", "expert"), None),
        P("section", ("groups", "expert"), None),
        P("section", "expert", None, "dp"),
        P("section", "expert", None, "dp"),
        P("section", "expert", "dp", None),
    )
    return jax.shard_map(
        on_device,
        mesh=mesh,
        in_specs=placed,
        out_specs=P("section", ("groups", "expert"), None),
        check_vma=False,
    )
```

profile of v0, /device:TPU:0, one launch (start us, length us, event | category | flops | bytes accessed | tf_op | source)
XLA Modules:
  0.0 225.6 jit_solution(16496183576223003052)
XLA Ops:
  0.0 0.8 copy.19
  0.8 0.1 eq.29
  0.9 0.1 eq.25
  1.0 0.7 broadcast_multiply_fusion
  1.7 1.1 reduce-window.6
  2.8 0.2 slice_reduce_fusion
  3.1 0.1 copy.18
  3.2 0.1 mul.52
  3.3 0.1 fusion.8
  3.4 2.4 %scatter_custom_fusion = s32[544]{0:T(1024)S(1)} fusion(s32[512]{0:T(512)S(1)} %bitcast.24, s32[512]{0:T(512)S(1)} %iota.11, s32[]{:T(128)} %constant.14.clone.1), kind=kCustom, calls=%fused_computation.41 | custom fusion | bytes 2180 | tf_op jit(solution)/shard_map/scatter | solution.py:61
  5.9 1.2 copy.21
  7.1 3.5 %gather_fusion = bf16[544,1440]{1,0:T(8,128)(2,1)} fusion(bf16[128,1440]{1,0:T(8,128)(2,1)S(1)} %bitcast.22, s32[1024]{0:T(1024)S(1)} %pad_clamp_fusion.1), kind=kCustom, calls=%fused_computation | custom fusion | bytes 3135616 | tf_op jit(solution)/shard_map/gather | solution.py:68
  10.6 1.8 gather.14
  12.4 0.2 copy.22
  12.6 3.5 %gather_fusion.1 = bf16[544,1440]{1,0:T(8,128)(2,1)} fusion(bf16[128,1440]{1,0:T(8,128)(2,1)S(1)} %bitcast.21, s32[1024]{0:T(1024)S(1)} %pad_clamp_fusion.1), kind=kCustom, calls=%fused_computation.1 | custom fusion | bytes 3135616 | tf_op jit(solution)/shard_map/gather | solution.py:65
  16.2 2.7 %gather.16 = bf16[16,34,1440]{2,1,0:T(8,128)(2,1)} reshape(bf16[544,1440]{1,0:T(8,128)(2,1)} %gather_fusion.1) | data formatting | bytes 3133440 | tf_op jit(solution)/shard_map/gather | solution.py:65
  18.9 0.1 broadcast_in_dim.33
  19.0 3.2 %broadcast_select_fusion = (bf16[16,34,1440]{2,1,0:T(8,128)(2,1)S(1)}, bf16[16,34,1440]{2,1,0:T(8,128)(2,1)}) fusion(bf16[16,34,1440]{2,1,0:T(8,128)(2,1)} %gather.16, pred[16,34]{1,0:T(8,128)(4,1)S(1)} %broadcast_in_dim.33, bf16[16,34,1440]{2,1,0:T(8,128)(2,1)S(1)} %gather.14), kind=kLoop, calls=%fused_computation.17 | loop fusion | flops 1566720 | bytes 6267424 | tf_op jit(solution)/shard_map/jit(_where)/select_n | solution.py:65
  22.1 52.3 %all_to_all.15 = bf16[16,34,1440]{2,1,0:T(8,128)(2,1)} all-to-all(bf16[16,34,1440]{2,1,0:T(8,128)(2,1)S(1)} %get-tuple-element.5), channel_id=1, replica_groups=mesh['groups'=1,'expert'=16,'section'=2,'dp'=1] {'expert'}, dimensions={0} | all-to-all | bytes 3133440 | tf_op jit(solution)/shard_map/all_to_all | solution.py:77
  74.5 4.5 %all-to-all-start = ((bf16[16,34,1440]{2,1,0:T(8,128)(2,1)}), bf16[16,34,1440]{2,1,0:T(8,128)(2,1)S(1)}, u32[]{:S(2)}, u32[]{:S(2)}) async-start(bf16[16,34,1440]{2,1,0:T(8,128)(2,1)} %get-tuple-element.6), calls=%async_computation | async-start | bytes 3932160 | tf_op jit(solution)/shard_map/all_to_all | solution.py:78
  79.0 0.4 collective-permute-start.2
  79.4 0.2 collective-permute-start
  79.6 0.3 collective-permute-start.1
  79.9 2.9 %reshape.96 = bf16[544,1440]{1,0:T(8,128)(2,1)} reshape(bf16[16,34,1440]{2,1,0:T(8,128)(2,1)} %all_to_all.15) | data formatting | bytes 3133440 | tf_op jit(solution)/shard_map/reshape | solution.py:81
  82.9 35.0 %all-to-all-done = bf16[16,34,1440]{2,1,0:T(8,128)(2,1)S(1)} async-done(((bf16[16,34,1440]{2,1,0:T(8,128)(2,1)}), bf16[16,34,1440]{2,1,0:T(8,128)(2,1)S(1)}, u32[]{:S(2)}, u32[]{:S(2)}) %all-to-all-start) | async-done | bytes 1566752 | tf_op jit(solution)/shard_map/all_to_all | solution.py:78
  117.8 1.7 reshape.95
  119.6 0.0 collective-permute-done.2
  119.6 5.7 %fusion.4 = f32[544,1440]{1,0:T(8,128)S(1)} fusion(bf16[544,1440]{1,0:T(8,128)(2,1)} %reshape.96, bf16[1440,720]{1,0:T(8,128)(2,1)} %collective-permute-done.2, bf16[1440,720]{1,0:T(8,128)(2,1)} %bitcast.33), kind=kOutput, calls=%fused_computation.15 | convolution fusion | flops 2264371200 | bytes 8847360 | tf_op jit(solution)/shard_map/dot_general | solution.py:22
  125.3 0.0 copy-start.6
  125.3 0.0 copy-start.5
  125.3 0.0 collective-permute-done
  125.3 5.6 %fusion = f32[544,1440]{1,0:T(8,128)S(1)} fusion(bf16[544,1440]{1,0:T(8,128)(2,1)S(1)} %copy-done.1, bf16[720,1440]{1,0:T(8,128)(2,1)} %collective-permute-done, bf16[720,1440]{1,0:T(8,128)(2,1)S(1)} %bitcast.28), kind=kOutput, calls=%fused_computation.4 | convolution fusion | flops 2264371200 | bytes 8847360 | tf_op jit(solution)/shard_map/dot_general | solution.py:24
  131.0 0.0 collective-permute-done.1
  131.0 1.7 copy-done.7
  132.8 6.3 %fusion.5 = f32[544,1440]{1,0:T(8,128)} fusion(bf16[1440,720]{1,0:T(8,128)(2,1)} %collective-permute-done.1, bf16[1440,720]{1,0:T(8,128)(2,1)S(1)} %bitcast.31, f32[544,1440]{1,0:T(8,128)S(1)} %fusion, f32[544,1440]{1,0:T(8,128)S(1)} %fusion.4), kind=kOutput, calls=%fused_computation.16 | convolution fusion | flops 2269854720 | bytes 13547520 | tf_op jit(solution)/shard_map/dot_general | solution.py:34
  139.1 12.3 %add_convert_fusion = bf16[544,1440]{1,0:T(8,128)(2,1)S(1)} fusion(f32[544,1440]{1,0:T(8,128)} %fusion.5, bf16[1440,720]{1,0:T(8,128)(2,1)} %collective-permute-done.2, bf16[1440,720]{1,0:T(8,128)(2,1)} %bitcast.34, f32[544,1440]{1,0:T(8,128)} %copy-done.7, bf16[544,1440]{1,0:T(8,128)(2,1)S(1)} %copy-done, f32[544,1440]{1,0:T(8,128)} %copy-done.6, ...), kind=kOutput, calls=%fused_computation.10 | convolution fusion | flops 4539709440 | bytes 20828160 | tf_op jit(solution)/shard_map/dot_general | solution.py:31
  151.4 0.0 copy-start.3
  151.4 1.6 reshape.97
  153.0 10.7 %all-to-all-start.2 = ((bf16[16,34,1440]{2,1,0:T(8,128)(2,1)}), bf16[16,34,1440]{2,1,0:T(8,128)(2,1)}, u32[]{:S(2)}, u32[]{:S(2)}) async-start(bf16[16,34,1440]{2,1,0:T(8,128)(2,1)} %reshape.97), calls=%async_computation.2 | async-start | bytes 3932160 | tf_op jit(solution)/shard_map/all_to_all | solution.py:88
  163.8 0.1 copy.17
  163.9 38.7 %all-to-all-done.2 = bf16[16,34,1440]{2,1,0:T(8,128)(2,1)} async-done(((bf16[16,34,1440]{2,1,0:T(8,128)(2,1)}), bf16[16,34,1440]{2,1,0:T(8,128)(2,1)}, u32[]{:S(2)}, u32[]{:S(2)}) %all-to-all-start.2) | async-done | bytes 1566752 | tf_op jit(solution)/shard_map/all_to_all | solution.py:88
  202.6 2.0 reshape.98
  204.7 3.0 %gather_fusion.2 = bf16[512,1440]{1,0:T(8,128)(2,1)} fusion(bf16[544,1440]{1,0:T(8,128)(2,1)S(1)} %reshape.98, s32[1024]{0:T(1024)S(1)} %pad_clamp_fusion), kind=kCustom, calls=%fused_computation.2 | custom fusion | bytes 2951168 | tf_op jit(solution)/shard_map/gather | solution.py:90
  207.6 2.9 %reshape.99 = f32[128,4,1440]{2,1,0:T(4,128)S(1)} reshape(bf16[512,1440]{1,0:T(8,128)(2,1)} %gather_fusion.2) | data formatting | bytes 4423680 | tf_op jit(solution)/shard_map/convert_element_type | solution.py:90
  210.5 2.2 multiply_reduce_fusion
  212.8 1.6 collective-permute-start.3
  214.4 10.3 %collective-permute-done.3 = bf16[128,1440]{1,0:T(8,128)(2,1)S(1)} collective-permute-done((bf16[128,1440]{1,0:T(8,128)(2,1)S(1)}, bf16[128,1440]{1,0:T(8,128)(2,1)S(1)}, u32[]{:S(2)}, u32[]{:S(2)}) %collective-permute-start.3) | collective-permute-done | bytes 368672 | tf_op jit(solution)/shard_map/ppermute | solution.py:18
  224.6 0.9 copy.23
  (23 shorter events, 0.1 us)
Async XLA Ops:
  10.6 1.8 copy-start.2
  74.5 43.4 %all-to-all-start = ((bf16[16,34,1440]{2,1,0:T(8,128)(2,1)}), bf16[16,34,1440]{2,1,0:T(8,128)(2,1)S(1)}, u32[]{:S(2)}, u32[]{:S(2)}) async-start(bf16[16,34,1440]{2,1,0:T(8,128)(2,1)} %get-tuple-element.6), calls=%async_computation | async-start | bytes 3932160 | tf_op jit(solution)/shard_map/all_to_all | solution.py:78
  79.0 40.6 %collective-permute-start.2 = (bf16[1440,720]{1,0:T(8,128)(2,1)}, bf16[1440,720]{1,0:T(8,128)(2,1)}, u32[]{:S(2)}, u32[]{:S(2)}) collective-permute-start(bf16[1440,720]{1,0:T(8,128)(2,1)} %bitcast.32), channel_id=1, source_target_pairs={{0,2},{2,0},{4,6},{6,4},{8,10},{10,8},{12,14},{14,12},{16,18},{18,... | collective-permute-start | bytes 6220808 | tf_op jit(solution)/shard_map/ppermute | solution.py:12
  79.4 45.9 %collective-permute-start = (bf16[720,1440]{1,0:T(8,128)(2,1)}, bf16[720,1440]{1,0:T(8,128)(2,1)}, u32[]{:S(2)}, u32[]{:S(2)}) collective-permute-start(bf16[720,1440]{1,0:T(8,128)(2,1)} %bitcast.27), channel_id=1, source_target_pairs={{0,2},{2,0},{4,6},{6,4},{8,10},{10,8},{12,14},{14,12},{16,18},{18,... | collective-permute-start | bytes 6220808 | tf_op jit(solution)/shard_map/ppermute | solution.py:12
  79.6 51.4 %collective-permute-start.1 = (bf16[1440,720]{1,0:T(8,128)(2,1)}, bf16[1440,720]{1,0:T(8,128)(2,1)}, u32[]{:S(2)}, u32[]{:S(2)}) collective-permute-start(bf16[1440,720]{1,0:T(8,128)(2,1)} %bitcast.29), channel_id=1, source_target_pairs={{0,2},{2,0},{4,6},{6,4},{8,10},{10,8},{12,14},{14,12},{16,18},{18,... | collective-permute-start | bytes 6220808 | tf_op jit(solution)/shard_map/ppermute | solution.py:12
  119.6 5.7 %copy-start.1 = (bf16[544,1440]{1,0:T(8,128)(2,1)S(1)}, bf16[544,1440]{1,0:T(8,128)(2,1)}, u32[]{:S(2)}) copy-start(bf16[544,1440]{1,0:T(8,128)(2,1)} %reshape.95) | copy-start | bytes 4700164
  119.6 5.7 %copy-start.4 = (bf16[1,1,720,1440]{3,2,1,0:T(8,128)(2,1)S(1)}, bf16[1,1,720,1440]{3,2,1,0:T(8,128)(2,1)}, u32[]{:S(2)}) copy-start(bf16[1,1,720,1440]{3,2,1,0:T(8,128)(2,1)} %param.13) | copy-start | bytes 6220804
  125.3 5.7 %copy-start.6 = (f32[544,1440]{1,0:T(8,128)}, f32[544,1440]{1,0:T(8,128)S(1)}, u32[]{:S(2)}) copy-start(f32[544,1440]{1,0:T(8,128)S(1)} %fusion.4) | copy-start | bytes 9400324
  125.3 7.5 %copy-start.5 = (bf16[1,1,1440,720]{3,2,1,0:T(8,128)(2,1)S(1)}, bf16[1,1,1440,720]{3,2,1,0:T(8,128)(2,1)}, u32[]{:S(2)}) copy-start(bf16[1,1,1440,720]{3,2,1,0:T(8,128)(2,1)} %param.12) | copy-start | bytes 6220804
  131.0 1.8 copy-start.7
  131.0 8.1 %copy-start = (bf16[544,1440]{1,0:T(8,128)(2,1)S(1)}, bf16[544,1440]{1,0:T(8,128)(2,1)}, u32[]{:S(2)}) copy-start(bf16[544,1440]{1,0:T(8,128)(2,1)} %reshape.96) | copy-start | bytes 4700164
  151.4 12.3 %copy-start.3 = (f32[1,128,4]{1,2,0:T(4,128)S(1)}, f32[1,128,4]{1,2,0:T(4,128)}, u32[]{:S(2)}) copy-start(f32[1,128,4]{1,2,0:T(4,128)} %param.10) | copy-start | bytes 6148
  153.0 49.6 %all-to-all-start.2 = ((bf16[16,34,1440]{2,1,0:T(8,128)(2,1)}), bf16[16,34,1440]{2,1,0:T(8,128)(2,1)}, u32[]{:S(2)}, u32[]{:S(2)}) async-start(bf16[16,34,1440]{2,1,0:T(8,128)(2,1)} %reshape.97), calls=%async_computation.2 | async-start | bytes 3932160 | tf_op jit(solution)/shard_map/all_to_all | solution.py:88
  212.8 11.9 %collective-permute-start.3 = (bf16[128,1440]{1,0:T(8,128)(2,1)S(1)}, bf16[128,1440]{1,0:T(8,128)(2,1)S(1)}, u32[]{:S(2)}, u32[]{:S(2)}) collective-permute-start(bf16[128,1440]{1,0:T(8,128)(2,1)S(1)} %multiply_reduce_fusion), channel_id=1, source_target_pairs={{1,0},{0,1},{3,2},{2,3},{5,4},{4,5},{7,6},{6,7},{9,8},{8,9},{11,10... | collective-permute-start | bytes 1105928 | tf_op jit(solution)/shard_map/ppermute | solution.py:18
where the time goes:
time: 230 us; the launch traced here: 226 us
  waiting for transfers between devices  84 us (37%)
  blocking collectives  52.3 us (23%)
  local copies, waits for them, and re-layouts  33.9 us (15%)
  matrix products  30 us (13%)
  starting transfers between devices  17.8 us (8%)
  other arithmetic  7.42 us (3%)
    all_to_all x1, blocking collectives, on_device(): lax.all_to_all(split_feats, 'expert', split_axis=0, concat_axis=0, tiled=...  52.3 us
    all_to_all x1, waiting for transfers between devices, on_device(): lax.all_to_all(result, 'expert', split_axis=0, concat_axis=0, tiled=True)  38.7 us
    all_to_all x1, waiting for transfers between devices, on_device(): lax.all_to_all(split_grads, 'expert', split_axis=0, concat_axis=0, tiled=...  35 us
    dot_general x1, matrix products, expert_rows(): lax.dot_general(gate_grad, gate_mat, (((1,), (1,)), ((), ())), preferred_...  12.3 us
    all_to_all x1, starting transfers between devices, on_device(): lax.all_to_all(result, 'expert', split_axis=0, concat_axis=0, tiled=True)  10.7 us
    ppermute x1, waiting for transfers between devices, shifted(): return lax.ppermute(block, axis, route)  10.3 us
    dot_general x1, matrix products, expert_rows(): lax.dot_general(up_grad, up_mat, (((1,), (1,)), ((), ())), preferred_elem...  6.34 us
    gather x2, local copies, waits for them, and re-layouts, on_device(): feat_rows[source]  6.26 us
  transfers between devices with their start and end apart: 6, of which 3 were waited for; matrix products, arithmetic and copies ran while one was open for 7% of the time, Pallas kernels for 0%

commit v1 on v0

--- a/solution.py
+++ b/solution.py
@@ -1,6 +1,10 @@
+import functools
+
 import jax
 import jax.numpy as jnp
 from jax import lax
+from jax.experimental import pallas as pl
+from jax.experimental.pallas import tpu as pltpu
 from jax.sharding import PartitionSpec as P
 
 swish_alpha = 1.702
@@ -95,6 +99,391 @@
     return passed[None]
 
 
+MESH = pl.DeviceIdType.MESH
+ROWS = 32
+
+
+def dot(a, b, ca=1, cb=0):
+    return lax.dot_general(a, b, (((ca,), (cb,)), ((), ())), preferred_element_type=jnp.float32)
+
+
+def chain_kernel(
+    n, sections, experts, cap,
+    ids_ref, logits_ref, feat_hbm, grad_hbm, gate_hbm, up_hbm, down_hbm, out_ref,
+    feat, grad, meta, rows_f, rows_g, send_f, send_g, res, res_in,
+    part, part_send, up_in, dn_in, gate, up, down,
+    own_sem, w_sem, w_send, w_recv,
+    ag_recv, ag_up, ag_dn, y_send, y_recv, r_send, r_recv,
+    p_send, up_recv, dn_recv, o_send, o_recv,
+):
+    top_count, tokens = ids_ref.shape
+    me = lax.axis_index("expert")
+    section = lax.axis_index("section")
+    core = lax.rem(me, 2)
+    e = me // 2
+    y = lax.rem(e, 2)
+    z = me // 4
+    e_nb = e + 1 - 2 * y
+    core_nb = {"expert": me + 1 - 2 * core}
+    y_nb = {"expert": me + 2 - 4 * y}
+    above, below = {"expert": me + 4}, {"expert": me - 4}
+    before = {"section": lax.rem(section + sections - 1, sections)}
+    after = {"section": lax.rem(section + 1, sections)}
+    has_up, has_dn = z < n - 1, z > 0
+
+    barrier = pltpu.get_barrier_semaphore()
+    for peer in (core_nb, y_nb, before, after):
+        pl.semaphore_signal(barrier, inc=1, device_id=peer, device_id_type=MESH)
+
+    @pl.when(has_up)
+    def _():
+        pl.semaphore_signal(barrier, inc=1, device_id=above, device_id_type=MESH)
+
+    @pl.when(has_dn)
+    def _():
+        pl.semaphore_signal(barrier, inc=1, device_id=below, device_id_type=MESH)
+
+    raised = jnp.exp(logits_ref[...])
+    weights = raised / jnp.sum(raised, axis=0, keepdims=True)
+    ids = ids_ref[...]
+    expert_row = lax.broadcasted_iota(jnp.int32, (experts, tokens), 0)
+    chosen = jnp.zeros((experts, tokens), jnp.float32)
+    weight = jnp.zeros((experts, tokens), jnp.float32)
+    for k in range(top_count):
+        hit = jnp.where(ids[k : k + 1, :] == expert_row, 1.0, 0.0)
+        chosen = chosen + hit
+        weight = weight + hit * weights[k : k + 1, :]
+    earlier = lax.broadcasted_iota(jnp.int32, (tokens, tokens), 0) < lax.broadcasted_iota(
+        jnp.int32, (tokens, tokens), 1
+    )
+    place = dot(chosen.astype(jnp.bfloat16), jnp.where(earlier, 1.0, 0.0).astype(jnp.bfloat16))
+    place = jnp.where(chosen > 0.5, place, -1.0)
+    meta[z, :experts, :] = weight
+    meta[z, experts:, :] = place
+
+    own_copies = [
+        pltpu.make_async_copy(feat_hbm.at[0], feat.at[z], own_sem.at[0]),
+        pltpu.make_async_copy(grad_hbm.at[0], grad.at[z], own_sem.at[1]),
+    ]
+    for copy in own_copies:
+        copy.start()
+    w_copies = [
+        pltpu.make_async_copy(src.at[0, 0], dst.at[0], w_sem.at[j])
+        for j, (src, dst) in enumerate(((gate_hbm, gate), (up_hbm, up), (down_hbm, down)))
+    ]
+    for copy in w_copies:
+        copy.start()
+
+    pl.semaphore_wait(
+        barrier, 4 + jnp.where(has_up, 1, 0) + jnp.where(has_dn, 1, 0)
+    )
+
+    def remote(src, dst, s_sem, r_sem, peer):
+        return pltpu.make_async_remote_copy(
+            src_ref=src, dst_ref=dst, send_sem=s_sem, recv_sem=r_sem,
+            device_id=peer, device_id_type=MESH,
+        )
+
+    buffers = (feat, grad, meta)
+
+    def hop(kind, b, upward, src=None):
+        buf = buffers[kind].at[b]
+        sems = ag_up if upward else ag_dn
+        return remote(
+            buf if src is None else src, buf, sems.at[kind, b], ag_recv.at[kind, b],
+            above if upward else below,
+        )
+
+    sources = (feat_hbm.at[0], grad_hbm.at[0], None)
+    for kind in (2, 0, 1):
+        @pl.when(has_up)
+        def _():
+            hop(kind, z, True, sources[kind]).start()
+
+        @pl.when(has_dn)
+        def _():
+            hop(kind, z, False, sources[kind]).start()
+
+    swaps = [
+        remote(src.at[0, 0], dst.at[1], w_send.at[j], w_recv.at[j], core_nb)
+        for j, (src, dst) in enumerate(((gate_hbm, gate), (up_hbm, up), (down_hbm, down)))
+    ]
+    for copy in swaps:
+        copy.start()
+
+    def block_of(k):
+        near = jnp.minimum(z, n - 1 - z)
+        half = (k + 1) // 2
+        side = jnp.where(lax.rem(k, 2) == 1, z - half, z + half)
+        far = jnp.where(z < n - 1 - z, z + k - near, z - k + near)
+        return jnp.where(k <= 2 * near, side, far)
+
+    def arrive(kind, b):
+        @pl.when(b != z)
+        def _():
+            hop(kind, b, True).wait_recv()
+
+        if kind < 2:
+            @pl.when(b == z)
+            def _():
+                own_copies[kind].wait()
+
+        @pl.when(jnp.logical_and(b < z, has_up))
+        def _():
+            hop(kind, b, True).start()
+
+        @pl.when(jnp.logical_and(b > z, has_dn))
+        def _():
+            hop(kind, b, False).start()
+
+    def y_copy(kind, b):
+        src, dst = ((send_f, rows_f), (send_g, rows_g))[kind]
+        return remote(
+            src.at[b], dst.at[b, pl.ds(cap, cap)], y_send.at[kind, b], y_recv.at[kind, b], y_nb
+        )
+
+    def picks(b, expert):
+        row = meta[b, pl.ds(experts + expert, 1), :]
+        slot = lax.broadcasted_iota(jnp.int32, (cap, tokens), 0).astype(jnp.float32)
+        return jnp.where(slot == row, 1.0, 0.0).astype(jnp.bfloat16)
+
+    def stage_a(k):
+        b = block_of(k)
+        arrive(2, b)
+        own, nb = picks(b, e), picks(b, e_nb)
+        for kind, (whole, rows, sent) in enumerate(
+            ((feat, rows_f, send_f), (grad, rows_g, send_g))
+        ):
+            arrive(kind, b)
+            values = whole[b]
+            sent[b] = dot(nb, values).astype(jnp.bfloat16)
+            y_copy(kind, b).start()
+            rows[b, :cap, :] = dot(own, values).astype(jnp.bfloat16)
+
+    def r_copy(b):
+        return remote(
+            res.at[b, pl.ds(cap, cap)], res_in.at[b], r_send.at[b], r_recv.at[b], y_nb
+        )
+
+    def stage_b(k):
+        b = block_of(k)
+
+        @pl.when(k == 0)
+        def _():
+            for copy in w_copies:
+                copy.wait()
+            for copy in swaps:
+                copy.wait_recv()
+
+        y_copy(0, b).wait_recv()
+        y_copy(1, b).wait_recv()
+
+        def one_half(h, total):
+            f, g = rows_f[b], rows_g[b]
+            gate_pre = dot(f, gate[h])
+            up_pre = dot(f, up[h])
+            hidden_grad = dot(g, down[h], 1, 1)
+            squash = jax.nn.sigmoid(swish_alpha * gate_pre)
+            slope = squash + swish_alpha * gate_pre * squash * (1.0 - squash)
+            gate_grad = (hidden_grad * (up_pre + 1.0) * slope).astype(jnp.bfloat16)
+            up_grad = (hidden_grad * gate_pre * squash).astype(jnp.bfloat16)
+            value = dot(gate_grad, gate[h], 1, 1) + dot(up_grad, up[h], 1, 1)
+            return value if total is None else total + value
+
+        total = one_half(1, one_half(0, None))
+        res[b] = total.astype(jnp.bfloat16)
+        r_copy(b).start()
+
+    def p_copy(b, r, upward):
+        rows = pl.ds(pl.multiple_of(r * ROWS, ROWS), ROWS)
+        dst, sems = (up_in, up_recv) if upward else (dn_in, dn_recv)
+        return remote(
+            part_send.at[b, rows], dst.at[b, rows], p_send.at[b, r], sems.at[b, r],
+            above if upward else below,
+        )
+
+    pieces = tokens // ROWS
+
+    def stage_c(k):
+        b = block_of(k)
+        r_copy(b).wait_recv()
+        rows = jnp.concatenate(
+            [
+                meta[b, pl.ds(e, 1), :],
+                meta[b, pl.ds(e_nb, 1), :],
+                jnp.zeros((6, tokens), jnp.float32),
+            ],
+            axis=0,
+        )
+        columns = rows.T
+        value = columns[:, 0:1] * dot(picks(b, e), res[b, :cap, :], 0, 0)
+        value = value + columns[:, 1:2] * dot(picks(b, e_nb), res_in[b], 0, 0)
+        part[b] = value
+        up_end = jnp.logical_and(b > z, jnp.logical_not(has_dn))
+        dn_end = jnp.logical_and(b < z, jnp.logical_not(has_up))
+
+        @pl.when(jnp.logical_or(up_end, dn_end))
+        def _():
+            part_send[b] = value.astype(jnp.bfloat16)
+
+        @pl.when(up_end)
+        def _():
+            @pl.loop(0, pieces)
+            def _(r):
+                p_copy(b, r, True).start()
+
+        @pl.when(dn_end)
+        def _():
+            @pl.loop(0, pieces)
+            def _(r):
+                p_copy(b, r, False).start()
+
+    @pl.loop(0, n + 2)
+    def _(k):
+        @pl.when(k < n)
+        def _():
+            stage_a(k)
+
+        @pl.when(jnp.logical_and(k >= 1, k <= n))
+        def _():
+            stage_b(k - 1)
+
+        @pl.when(k >= 2)
+        def _():
+            stage_c(k - 2)
+
+    def pass_on(b, upward):
+        incoming = up_in if upward else dn_in
+
+        @pl.loop(0, pieces)
+        def _(r):
+            rows = pl.ds(pl.multiple_of(r * ROWS, ROWS), ROWS)
+            p_copy(b, r, upward).wait_recv()
+            value = part[b, rows, :] + incoming[b, rows, :].astype(jnp.float32)
+            part_send[b, rows, :] = value.astype(jnp.bfloat16)
+            p_copy(b, r, upward).start()
+
+    @pl.loop(0, n)
+    def _(j):
+        b = n - 1 - j
+
+        @pl.when(jnp.logical_and(b > z, has_dn))
+        def _():
+            pass_on(b, True)
+
+    @pl.loop(0, n)
+    def _(b):
+        @pl.when(jnp.logical_and(b < z, has_up))
+        def _():
+            pass_on(b, False)
+
+    def o_copy(r):
+        rows = pl.ds(pl.multiple_of(r * ROWS, ROWS), ROWS)
+        return remote(
+            part_send.at[z, rows], out_ref.at[0, rows], o_send.at[r], o_recv.at[r], before
+        )
+
+    @pl.loop(0, pieces)
+    def _(r):
+        rows = pl.ds(pl.multiple_of(r * ROWS, ROWS), ROWS)
+
+        @pl.when(has_dn)
+        def _():
+            p_copy(z, r, True).wait_recv()
+            part[z, rows, :] += up_in[z, rows, :].astype(jnp.float32)
+
+        @pl.when(has_up)
+        def _():
+            p_copy(z, r, False).wait_recv()
+            part[z, rows, :] += dn_in[z, rows, :].astype(jnp.float32)
+
+        part_send[z, rows, :] = part[z, rows, :].astype(jnp.bfloat16)
+        o_copy(r).start()
+
+    for copy in swaps:
+        copy.wait_send()
+
+    @pl.loop(0, n)
+    def _(b):
+        @pl.when(jnp.logical_and(b <= z, has_up))
+        def _():
+            for kind in range(3):
+                hop(kind, b, True).wait_send()
+
+        @pl.when(jnp.logical_and(b >= z, has_dn))
+        def _():
+            for kind in range(3):
+                hop(kind, b, False).wait_send()
+
+        y_copy(0, b).wait_send()
+        y_copy(1, b).wait_send()
+        r_copy(b).wait_send()
+
+        @pl.when(b != z)
+        def _():
+            @pl.loop(0, pieces)
+            def _(r):
+                p_copy(b, r, True).wait_send()
+
+    @pl.loop(0, pieces)
+    def _(r):
+        o_copy(r).wait_send()
+        o_copy(r).wait_recv()
+
+
+def chained(saved_input, grad_output, expert_ids, router_logits, w_gate, w_up, w_down):
+    _, tokens, features = saved_input.shape
+    half = w_gate.shape[3]
+    top_count = expert_ids.shape[2]
+    slices = lax.axis_size("expert")
+    experts = slices // 2
+    n = slices // 4
+    sections = lax.axis_size("section")
+    capacity = min(tokens, tokens * top_count // experts * 17 // 16 // 2 * 2)
+    cap = -(-capacity // 16) * 16
+    pieces = tokens // ROWS
+    bf16 = jnp.bfloat16
+    dma = pltpu.SemaphoreType.DMA
+    vmem, anywhere = pl.BlockSpec(memory_space=pltpu.VMEM), pl.BlockSpec(memory_space=pl.ANY)
+    macs = 5 * 2 * n * cap * features * 2 * half
+    return pl.pallas_call(
+        functools.partial(chain_kernel, n, sections, experts, cap),
+        out_shape=jax.ShapeDtypeStruct((1, tokens, features), bf16),
+        in_specs=[vmem, vmem] + [anywhere] * 5,
+        out_specs=anywhere,
+        scratch_shapes=[
+            pltpu.VMEM((n, tokens, features), bf16),
+            pltpu.VMEM((n, tokens, features), bf16),
+            pltpu.VMEM((n, 2 * experts, tokens), jnp.float32),
+            pltpu.VMEM((n, 2 * cap, features), bf16),
+            pltpu.VMEM((n, 2 * cap, features), bf16),
+            pltpu.VMEM((n, cap, features), bf16),
+            pltpu.VMEM((n, cap, features), bf16),
+            pltpu.VMEM((n, 2 * cap, features), bf16),
+            pltpu.VMEM((n, cap, features), bf16),
+            pltpu.VMEM((n, tokens, features), jnp.float32),
+            pltpu.VMEM((n, tokens, features), bf16),
+            pltpu.VMEM((n, tokens, features), bf16),
+            pltpu.VMEM((n, tokens, features), bf16),
+            pltpu.VMEM((2, features, half), bf16),
+            pltpu.VMEM((2, features, half), bf16),
+            pltpu.VMEM((2, half, features), bf16),
+            dma((2,)), dma((3,)), dma((3,)), dma((3,)),
+            dma((3, n)), dma((3, n)), dma((3, n)),
+            dma((2, n)), dma((2, n)), dma((n,)), dma((n,)),
+            dma((n, pieces)), dma((n, pieces)), dma((n, pieces)),
+            dma((pieces,)), dma((pieces,)),
+        ],
+        compiler_params=pltpu.CompilerParams(
+            collective_id=0, has_side_effects=True, vmem_limit_bytes=58 * 1024 * 1024
+        ),
+        cost_estimate=pl.CostEstimate(
+            flops=2 * macs, bytes_accessed=6 * half * features + 6 * tokens * features,
+            transcendentals=4 * n * cap * half,
+        ),
+    )(expert_ids[0].T, router_logits[0].T, saved_input, grad_output, w_gate, w_up, w_down)
+
+
 def solution(mesh):
     placed = (
         P("section", ("groups", "expert"), None),
@@ -105,8 +494,10 @@
         P("section", "expert", None, "dp"),
         P("section", "expert", "dp", None),
     )
+    shape = dict(mesh.shape)
+    chain = shape["dp"] == 1 and shape["expert"] % 4 == 0 and shape["section"] > 1
     return jax.shard_map(
-        on_device,
+        chained if chain else on_device,
         mesh=mesh,
         in_specs=placed,
         out_specs=P("section", ("groups", "expert"), None),

time: 230 us -> 125 us (0.54); the launches traced: 226 us -> 125 us
  Pallas kernels: 0 us -> 119 us
  waiting for transfers between devices: 84 us -> 0 us
  blocking collectives: 52.3 us -> 0 us
  matrix products: 30 us -> 0 us
  local copies, waits for them, and re-layouts: 33.9 us -> 5.72 us
  starting transfers between devices: 17.8 us -> 0 us
  other arithmetic: 7.42 us -> 0 us
    pallas_call x0 -> x1, Pallas kernels: none -> 119 us  [chained(): pl.pallas_call(functools.partial(chain_kernel, n, sections, experts, cap)...]
    all_to_all x2 -> x0, waiting for transfers between devices: 73.7 us -> none  [the longest x1 38.7 us: on_device(): lax.all_to_all(result, 'expert', split_axis=0, concat_axis=0, tiled=True)]
    all_to_all x1 -> x0, blocking collectives: 52.3 us -> none  [on_device(): lax.all_to_all(split_feats, 'expert', split_axis=0, concat_axis=0, tiled=...]
    dot_general x4 -> x0, matrix products: 30 us -> none  [the longest x1 12.3 us: expert_rows(): lax.dot_general(gate_grad, gate_mat, (((1,), (1,)), ((), ())), preferred_...]
    all_to_all x2 -> x0, starting transfers between devices: 15.3 us -> none  [the longest x1 10.7 us: on_device(): lax.all_to_all(result, 'expert', split_axis=0, concat_axis=0, tiled=True)]
    gather x5 -> x0, local copies, waits for them, and re-layouts: 14.5 us -> none  [the longest x2 6.26 us: on_device(): feat_rows[source]]
    ppermute x4 -> x0, waiting for transfers between devices: 10.3 us -> none  [the longest x1 10.3 us: shifted(): return lax.ppermute(block, axis, route)]
    reshape x4 -> x0, local copies, waits for them, and re-layouts: 8.28 us -> none  [the longest x1 2.95 us: on_device(): got_feats.reshape(-1, features)]
  transfers between devices with their start and end apart: 6 -> 0, of which waited for: 3 -> 0; matrix products, arithmetic and copies ran while one was open for 7% -> 0% of each run, Pallas kernels for 0% -> 0%
where the time goes in v1:
time: 125 us
  Pallas kernels  119 us (95%)
  local copies, waits for them, and re-layouts  5.72 us (5%)
    pallas_call x1, Pallas kernels, chained(): pl.pallas_call(functools.partial(chain_kernel, n, sections, experts, cap)...  119 us
    unnamed x2, local copies, waits for them, and re-layouts  3.8 us

profile of v1, /device:TPU:0, one launch (start us, length us, event | category | flops | bytes accessed | tf_op | source)
XLA Modules:
  0.0 125.1 jit_solution(10801169712120340264)
XLA Ops:
  0.0 1.9 %copy.8.feat_hbm = bf16[1,128,1440]{2,1,0:T(8,128)(2,1)} copy(bf16[1,128,1440]{1,2,0:T(8,128)(2,1)} %param.7) | data formatting | bytes 737280 | tf_op args[0]
  1.9 1.9 %copy.9.grad_hbm = bf16[1,128,1440]{2,1,0:T(8,128)(2,1)} copy(bf16[1,128,1440]{1,2,0:T(8,128)(2,1)} %param.8) | data formatting | bytes 737280 | tf_op args[1]
  3.8 119.4 %shard_map.73 = bf16[1,128,1440]{2,1,0:T(8,128)(2,1)} custom-call(s32[4,128]{1,0:T(4,128)} %bitcast.6, f32[4,128]{1,0:T(4,128)} %bitcast.7, bf16[1,128,1440]{2,1,0:T(8,128)(2,1)} %copy.8.feat_hbm, bf16[1,128,1440]{2,1,0:T(8,128)(2,1)} %copy.9.grad_hbm, bf16[1,1,1440,720]{3,2,1,0:T(8,128)(2,1)} %gate_hbm.1, bf16[1,1,1440,720]{3,2,1,0:T(8,128)(2,1)} %up_hbm.1, ...), custom_call_target="tpu_custom_call" | custom-call | flops 13271040000 | bytes 7326720 | tf_op jit(solution)/shard_map/pallas_call | solution.py:449
  123.2 1.9 %copy.10 = bf16[1,128,1440]{1,2,0:T(8,128)(2,1)} copy(bf16[1,128,1440]{2,1,0:T(8,128)(2,1)} %shard_map.73) | data formatting | bytes 737280 | tf_op jit(solution)/shard_map/pallas_call | solution.py:449

commit v2 on v1

--- a/solution.py
+++ b/solution.py
@@ -100,7 +100,6 @@
 
 
 MESH = pl.DeviceIdType.MESH
-ROWS = 32
 
 
 def dot(a, b, ca=1, cb=0):
@@ -108,7 +107,7 @@
 
 
 def chain_kernel(
-    n, sections, experts, cap,
+    n, sections, experts, cap, pieces,
     ids_ref, logits_ref, feat_hbm, grad_hbm, gate_hbm, up_hbm, down_hbm, out_ref,
     feat, grad, meta, rows_f, rows_g, send_f, send_g, res, res_in,
     part, part_send, up_in, dn_in, gate, up, down,
@@ -117,6 +116,7 @@
     p_send, up_recv, dn_recv, o_send, o_recv,
 ):
     top_count, tokens = ids_ref.shape
+    features = feat_hbm.shape[0]
     me = lax.axis_index("expert")
     section = lax.axis_index("section")
     core = lax.rem(me, 2)
@@ -130,6 +130,7 @@
     before = {"section": lax.rem(section + sections - 1, sections)}
     after = {"section": lax.rem(section + 1, sections)}
     has_up, has_dn = z < n - 1, z > 0
+    size = features // pieces
 
     barrier = pltpu.get_barrier_semaphore()
     for peer in (core_nb, y_nb, before, after):
@@ -162,8 +163,8 @@
     meta[z, experts:, :] = place
 
     own_copies = [
-        pltpu.make_async_copy(feat_hbm.at[0], feat.at[z], own_sem.at[0]),
-        pltpu.make_async_copy(grad_hbm.at[0], grad.at[z], own_sem.at[1]),
+        pltpu.make_async_copy(feat_hbm, feat.at[z], own_sem.at[0]),
+        pltpu.make_async_copy(grad_hbm, grad.at[z], own_sem.at[1]),
     ]
     for copy in own_copies:
         copy.start()
@@ -194,7 +195,7 @@
             above if upward else below,
         )
 
-    sources = (feat_hbm.at[0], grad_hbm.at[0], None)
+    sources = (feat_hbm, grad_hbm, None)
     for kind in (2, 0, 1):
         @pl.when(has_up)
         def _():
@@ -218,23 +219,47 @@
         far = jnp.where(z < n - 1 - z, z + k - near, z - k + near)
         return jnp.where(k <= 2 * near, side, far)
 
+    def passes(b):
+        return jnp.logical_or(
+            jnp.logical_and(b < z, has_up), jnp.logical_and(b > z, has_dn)
+        )
+
+    def forward(kind, k):
+        b = block_of(k)
+
+        @pl.when(passes(b))
+        def _():
+            if kind == 0:
+                hop(2, b, True).wait_recv()
+            hop(kind, b, True).wait_recv()
+
+        for upward, there in ((True, jnp.logical_and(b < z, has_up)),
+                              (False, jnp.logical_and(b > z, has_dn))):
+            @pl.when(there)
+            def _():
+                if kind == 0:
+                    hop(2, b, upward).start()
+                hop(kind, b, upward).start()
+
+    def forwards(kind, k):
+        @pl.when(k == 1)
+        def _():
+            forward(kind, 1)
+
+        @pl.when(jnp.logical_and(k >= 1, k < n - 1))
+        def _():
+            forward(kind, k + 1)
+
     def arrive(kind, b):
-        @pl.when(b != z)
-        def _():
+        @pl.when(jnp.logical_and(b != z, jnp.logical_not(passes(b))))
+        def _():
+            if kind == 0:
+                hop(2, b, True).wait_recv()
             hop(kind, b, True).wait_recv()
 
-        if kind < 2:
-            @pl.when(b == z)
-            def _():
-                own_copies[kind].wait()
-
-        @pl.when(jnp.logical_and(b < z, has_up))
-        def _():
-            hop(kind, b, True).start()
-
-        @pl.when(jnp.logical_and(b > z, has_dn))
-        def _():
-            hop(kind, b, False).start()
+        @pl.when(b == z)
+        def _():
+            own_copies[kind].wait()
 
     def y_copy(kind, b):
         src, dst = ((send_f, rows_f), (send_g, rows_g))[kind]
@@ -247,18 +272,14 @@
         slot = lax.broadcasted_iota(jnp.int32, (cap, tokens), 0).astype(jnp.float32)
         return jnp.where(slot == row, 1.0, 0.0).astype(jnp.bfloat16)
 
-    def stage_a(k):
+    def stage_a(kind, k):
         b = block_of(k)
-        arrive(2, b)
-        own, nb = picks(b, e), picks(b, e_nb)
-        for kind, (whole, rows, sent) in enumerate(
-            ((feat, rows_f, send_f), (grad, rows_g, send_g))
-        ):
-            arrive(kind, b)
-            values = whole[b]
-            sent[b] = dot(nb, values).astype(jnp.bfloat16)
-            y_copy(kind, b).start()
-            rows[b, :cap, :] = dot(own, values).astype(jnp.bfloat16)
+        whole, rows, sent = ((feat, rows_f, send_f), (grad, rows_g, send_g))[kind]
+        arrive(kind, b)
+        values = whole[b]
+        sent[b] = dot(picks(b, e_nb), values, 1, 1).astype(jnp.bfloat16)
+        y_copy(kind, b).start()
+        rows[b, :cap, :] = dot(picks(b, e), values, 1, 1).astype(jnp.bfloat16)
 
     def r_copy(b):
         return remote(
@@ -295,29 +316,18 @@
         r_copy(b).start()
 
     def p_copy(b, r, upward):
-        rows = pl.ds(pl.multiple_of(r * ROWS, ROWS), ROWS)
+        rows = pl.ds(pl.multiple_of(r * size, size), size)
         dst, sems = (up_in, up_recv) if upward else (dn_in, dn_recv)
         return remote(
             part_send.at[b, rows], dst.at[b, rows], p_send.at[b, r], sems.at[b, r],
             above if upward else below,
         )
 
-    pieces = tokens // ROWS
-
     def stage_c(k):
         b = block_of(k)
         r_copy(b).wait_recv()
-        rows = jnp.concatenate(
-            [
-                meta[b, pl.ds(e, 1), :],
-                meta[b, pl.ds(e_nb, 1), :],
-                jnp.zeros((6, tokens), jnp.float32),
-            ],
-            axis=0,
-        )
-        columns = rows.T
-        value = columns[:, 0:1] * dot(picks(b, e), res[b, :cap, :], 0, 0)
-        value = value + columns[:, 1:2] * dot(picks(b, e_nb), res_in[b], 0, 0)
+        value = meta[b, pl.ds(e, 1), :] * dot(res[b, :cap, :], picks(b, e), 0, 0)
+        value = value + meta[b, pl.ds(e_nb, 1), :] * dot(res_in[b], picks(b, e_nb), 0, 0)
         part[b] = value
         up_end = jnp.logical_and(b > z, jnp.logical_not(has_dn))
         dn_end = jnp.logical_and(b < z, jnp.logical_not(has_up))
@@ -340,52 +350,69 @@
 
     @pl.loop(0, n + 2)
     def _(k):
+        forwards(0, k)
+
         @pl.when(k < n)
         def _():
-            stage_a(k)
+            stage_a(0, k)
+
+        @pl.when(k >= 2)
+        def _():
+            stage_c(k - 2)
 
         @pl.when(jnp.logical_and(k >= 1, k <= n))
         def _():
             stage_b(k - 1)
 
-        @pl.when(k >= 2)
-        def _():
-            stage_c(k - 2)
+        forwards(1, k)
+
+        @pl.when(k < n)
+        def _():
+            stage_a(1, k)
 
     def pass_on(b, upward):
         incoming = up_in if upward else dn_in
 
         @pl.loop(0, pieces)
         def _(r):
-            rows = pl.ds(pl.multiple_of(r * ROWS, ROWS), ROWS)
+            rows = pl.ds(pl.multiple_of(r * size, size), size)
             p_copy(b, r, upward).wait_recv()
             value = part[b, rows, :] + incoming[b, rows, :].astype(jnp.float32)
             part_send[b, rows, :] = value.astype(jnp.bfloat16)
             p_copy(b, r, upward).start()
 
+    def pass_up():
+        @pl.loop(0, n)
+        def _(b):
+            @pl.when(jnp.logical_and(b > z, has_dn))
+            def _():
+                pass_on(b, True)
+
+    @pl.when(z < n // 2)
+    def _():
+        pass_up()
+
     @pl.loop(0, n)
     def _(j):
         b = n - 1 - j
 
-        @pl.when(jnp.logical_and(b > z, has_dn))
-        def _():
-            pass_on(b, True)
-
-    @pl.loop(0, n)
-    def _(b):
         @pl.when(jnp.logical_and(b < z, has_up))
         def _():
             pass_on(b, False)
 
+    @pl.when(z >= n // 2)
+    def _():
+        pass_up()
+
     def o_copy(r):
-        rows = pl.ds(pl.multiple_of(r * ROWS, ROWS), ROWS)
+        rows = pl.ds(pl.multiple_of(r * size, size), size)
         return remote(
-            part_send.at[z, rows], out_ref.at[0, rows], o_send.at[r], o_recv.at[r], before
+            part_send.at[z, rows], out_ref.at[rows], o_send.at[r], o_recv.at[r], before
         )
 
     @pl.loop(0, pieces)
     def _(r):
-        rows = pl.ds(pl.multiple_of(r * ROWS, ROWS), ROWS)
+        rows = pl.ds(pl.multiple_of(r * size, size), size)
 
         @pl.when(has_dn)
         def _():
@@ -441,19 +468,19 @@
     sections = lax.axis_size("section")
     capacity = min(tokens, tokens * top_count // experts * 17 // 16 // 2 * 2)
     cap = -(-capacity // 16) * 16
-    pieces = tokens // ROWS
+    pieces = max(p for p in range(1, 7) if features % (16 * p) == 0)
     bf16 = jnp.bfloat16
     dma = pltpu.SemaphoreType.DMA
     vmem, anywhere = pl.BlockSpec(memory_space=pltpu.VMEM), pl.BlockSpec(memory_space=pl.ANY)
     macs = 5 * 2 * n * cap * features * 2 * half
-    return pl.pallas_call(
-        functools.partial(chain_kernel, n, sections, experts, cap),
-        out_shape=jax.ShapeDtypeStruct((1, tokens, features), bf16),
+    passed = pl.pallas_call(
+        functools.partial(chain_kernel, n, sections, experts, cap, pieces),
+        out_shape=jax.ShapeDtypeStruct((features, tokens), bf16),
         in_specs=[vmem, vmem] + [anywhere] * 5,
         out_specs=anywhere,
         scratch_shapes=[
-            pltpu.VMEM((n, tokens, features), bf16),
-            pltpu.VMEM((n, tokens, features), bf16),
+            pltpu.VMEM((n, features, tokens), bf16),
+            pltpu.VMEM((n, features, tokens), bf16),
             pltpu.VMEM((n, 2 * experts, tokens), jnp.float32),
             pltpu.VMEM((n, 2 * cap, features), bf16),
             pltpu.VMEM((n, 2 * cap, features), bf16),
@@ -461,10 +488,10 @@
             pltpu.VMEM((n, cap, features), bf16),
             pltpu.VMEM((n, 2 * cap, features), bf16),
             pltpu.VMEM((n, cap, features), bf16),
-            pltpu.VMEM((n, tokens, features), jnp.float32),
-            pltpu.VMEM((n, tokens, features), bf16),
-            pltpu.VMEM((n, tokens, features), bf16),
-            pltpu.VMEM((n, tokens, features), bf16),
+            pltpu.VMEM((n, features, tokens), jnp.float32),
+            pltpu.VMEM((n, features, tokens), bf16),
+            pltpu.VMEM((n, features, tokens), bf16),
+            pltpu.VMEM((n, features, tokens), bf16),
             pltpu.VMEM((2, features, half), bf16),
             pltpu.VMEM((2, features, half), bf16),
             pltpu.VMEM((2, half, features), bf16),
@@ -481,7 +508,11 @@
             flops=2 * macs, bytes_accessed=6 * half * features + 6 * tokens * features,
             transcendentals=4 * n * cap * half,
         ),
-    )(expert_ids[0].T, router_logits[0].T, saved_input, grad_output, w_gate, w_up, w_down)
+    )(
+        expert_ids[0].T, router_logits[0].T, saved_input[0].T, grad_output[0].T,
+        w_gate, w_up, w_down,
+    )
+    return passed.T[None]
 
 
 def solution(mesh):

time: 125 us -> 100 us (0.80)
  Pallas kernels: 119 us -> 98.1 us
  local copies, waits for them, and re-layouts: 5.72 us -> 1.75 us
    pallas_call x1, Pallas kernels: 119 us -> 98.1 us  [chained(): pl.pallas_call(functools.partial(chain_kernel, n, sections, experts, cap,...]
    unnamed x2 -> x1, local copies, waits for them, and re-layouts: 3.8 us -> 1.75 us
    pallas_call x1 -> x0, local copies, waits for them, and re-layouts: 1.91 us -> none  [chained(): pl.pallas_call(functools.partial(chain_kernel, n, sections, experts, cap)...]
where the time goes in v2:
time: 100 us; the launch traced here: 99.9 us
  Pallas kernels  98.1 us (98%)
  local copies, waits for them, and re-layouts  1.75 us (2%)
    pallas_call x1, Pallas kernels, chained(): pl.pallas_call(functools.partial(chain_kernel, n, sections, experts, cap,...  98.1 us

profile of v2, /device:TPU:0, one launch (start us, length us, event | category | flops | bytes accessed | tf_op | source)
XLA Modules:
  0.0 99.9 jit_solution(7050839888765465869)
XLA Ops:
  0.0 98.1 %shard_map.73 = bf16[1440,128]{1,0:T(8,128)(2,1)} custom-call(s32[4,128]{1,0:T(4,128)} %bitcast.18, f32[4,128]{1,0:T(4,128)} %bitcast.19, bf16[1440,128]{1,0:T(8,128)(2,1)} %bitcast.16, bf16[1440,128]{1,0:T(8,128)(2,1)} %bitcast.17, bf16[1,1,1440,720]{3,2,1,0:T(8,128)(2,1)} %gate_hbm.1, bf16[1,1,1440,720]{3,2,1,0:T(8,128)(2,1)} %up_hbm.1, ...), custom_call_target="tpu_custom_call" | custom-call | flops 13271040000 | bytes 7326720 | tf_op jit(solution)/shard_map/pallas_call | solution.py:476
  98.1 1.7 %copy.9 = bf16[1,128,1440]{1,2,0:T(8,128)(2,1)} copy(bf16[1,128,1440]{1,2,0:T(8,128)(2,1)} %bitcast.15) | data formatting | bytes 737280

commit v3 on v2

--- a/solution.py
+++ b/solution.py
@@ -110,7 +110,7 @@
     n, sections, experts, cap, pieces,
     ids_ref, logits_ref, feat_hbm, grad_hbm, gate_hbm, up_hbm, down_hbm, out_ref,
     feat, grad, meta, rows_f, rows_g, send_f, send_g, res, res_in,
-    part, part_send, up_in, dn_in, gate, up, down,
+    part, part_send, up_in, dn_in, gate, up, down, for_gate, for_up,
     own_sem, w_sem, w_send, w_recv,
     ag_recv, ag_up, ag_dn, y_send, y_recv, r_send, r_recv,
     p_send, up_recv, dn_recv, o_send, o_recv,
@@ -286,32 +286,38 @@
             res.at[b, pl.ds(cap, cap)], res_in.at[b], r_send.at[b], r_recv.at[b], y_nb
         )
 
-    def stage_b(k):
+    def weights_in(k, which):
+        @pl.when(k == 0)
+        def _():
+            for j in which:
+                w_copies[j].wait()
+            for j in which:
+                swaps[j].wait_recv()
+
+    def stage_bf(k):
         b = block_of(k)
-
-        @pl.when(k == 0)
-        def _():
-            for copy in w_copies:
-                copy.wait()
-            for copy in swaps:
-                copy.wait_recv()
-
+        weights_in(k, (0, 1))
         y_copy(0, b).wait_recv()
-        y_copy(1, b).wait_recv()
-
-        def one_half(h, total):
-            f, g = rows_f[b], rows_g[b]
+        for h in range(2):
+            f = rows_f[b]
             gate_pre = dot(f, gate[h])
             up_pre = dot(f, up[h])
-            hidden_grad = dot(g, down[h], 1, 1)
             squash = jax.nn.sigmoid(swish_alpha * gate_pre)
             slope = squash + swish_alpha * gate_pre * squash * (1.0 - squash)
-            gate_grad = (hidden_grad * (up_pre + 1.0) * slope).astype(jnp.bfloat16)
-            up_grad = (hidden_grad * gate_pre * squash).astype(jnp.bfloat16)
+            for_gate[h] = (up_pre + 1.0) * slope
+            for_up[h] = gate_pre * squash
+
+    def stage_bg(k):
+        b = block_of(k)
+        weights_in(k, (2,))
+        y_copy(1, b).wait_recv()
+        total = None
+        for h in range(2):
+            hidden_grad = dot(rows_g[b], down[h], 1, 1)
+            gate_grad = (hidden_grad * for_gate[h]).astype(jnp.bfloat16)
+            up_grad = (hidden_grad * for_up[h]).astype(jnp.bfloat16)
             value = dot(gate_grad, gate[h], 1, 1) + dot(up_grad, up[h], 1, 1)
-            return value if total is None else total + value
-
-        total = one_half(1, one_half(0, None))
+            total = value if total is None else total + value
         res[b] = total.astype(jnp.bfloat16)
         r_copy(b).start()
 
@@ -348,7 +354,7 @@
             def _(r):
                 p_copy(b, r, False).start()
 
-    @pl.loop(0, n + 2)
+    @pl.loop(0, n + 1)
     def _(k):
         forwards(0, k)
 
@@ -356,19 +362,20 @@
         def _():
             stage_a(0, k)
 
-        @pl.when(k >= 2)
-        def _():
-            stage_c(k - 2)
-
-        @pl.when(jnp.logical_and(k >= 1, k <= n))
-        def _():
-            stage_b(k - 1)
+        @pl.when(k >= 1)
+        def _():
+            stage_bg(k - 1)
 
         forwards(1, k)
 
         @pl.when(k < n)
         def _():
             stage_a(1, k)
+            stage_bf(k)
+
+        @pl.when(k >= 1)
+        def _():
+            stage_c(k - 1)
 
     def pass_on(b, upward):
         incoming = up_in if upward else dn_in
@@ -495,6 +502,8 @@
             pltpu.VMEM((2, features, half), bf16),
             pltpu.VMEM((2, features, half), bf16),
             pltpu.VMEM((2, half, features), bf16),
+            pltpu.VMEM((2, 2 * cap, half), jnp.float32),
+            pltpu.VMEM((2, 2 * cap, half), jnp.float32),
             dma((2,)), dma((3,)), dma((3,)), dma((3,)),
             dma((3, n)), dma((3, n)), dma((3, n)),
             dma((2, n)), dma((2, n)), dma((n,)), dma((n,)),

time: 100 us -> 99.3 us (level)
  no operation moved by 1% of the time
where the time goes in v3:
time: 99.3 us; the launch traced here: 99.1 us
  Pallas kernels  97.3 us (98%)
  local copies, waits for them, and re-layouts  1.75 us (2%)
    pallas_call x1, Pallas kernels, chained(): pl.pallas_call(functools.partial(chain_kernel, n, sections, experts, cap,...  97.3 us

profile of v3, /device:TPU:0, one launch (start us, length us, event | category | flops | bytes accessed | tf_op | source)
XLA Modules:
  0.0 99.1 jit_solution(6493569746853481889)
XLA Ops:
  0.0 97.3 %shard_map.73 = bf16[1440,128]{1,0:T(8,128)(2,1)} custom-call(s32[4,128]{1,0:T(4,128)} %bitcast.18, f32[4,128]{1,0:T(4,128)} %bitcast.19, bf16[1440,128]{1,0:T(8,128)(2,1)} %bitcast.16, bf16[1440,128]{1,0:T(8,128)(2,1)} %bitcast.17, bf16[1,1,1440,720]{3,2,1,0:T(8,128)(2,1)} %gate_hbm.1, bf16[1,1,1440,720]{3,2,1,0:T(8,128)(2,1)} %up_hbm.1, ...), custom_call_target="tpu_custom_call" | custom-call | flops 13271040000 | bytes 7326720 | tf_op jit(solution)/shard_map/pallas_call | solution.py:483
  97.4 1.7 %copy.9 = bf16[1,128,1440]{1,2,0:T(8,128)(2,1)} copy(bf16[1,128,1440]{1,2,0:T(8,128)(2,1)} %bitcast.15) | data formatting | bytes 737280
